TPU v7x, 256 devices: a whole 4x4x8 slice. The times are simulated.
256 devices in a mesh: exp: 64 (over z, y, core), voc: 4 (over x).
Axes of the slice: x: 4, y: 4, z: 8, core: 2. Of those that a mesh axis runs over, the one named last changes fastest.
Arguments:
- tokens: bfloat16 [2048, 4096], P('exp', 'voc'), may hold values from -6 to 6
- expert_routes: int32 [2048, 2], P('exp'), may hold values from 0 to 7, all different within a row; in each aligned block of 32 rows (0 to 31, 32 to 63, ...) at most 16 rows name the same one
- gate_scores: float32 [2048, 2], P('exp'), may hold values from 0.2 to 1
- w_gate: bfloat16 [64, 4096, 1792], P('exp', None, 'voc'), may hold values from -0.09375 to 0.09375
- w_up: bfloat16 [64, 4096, 1792], P('exp', None, 'voc'), may hold values from -0.09375 to 0.09375
- w_down: bfloat16 [64, 1792, 4096], P('exp', 'voc'), may hold values from -0.046875 to 0.046875
- head_weight: bfloat16 [4096, 32000], P('voc', 'exp'), may hold values from -0.09375 to 0.09375
- passage_ids: int32 [64, 32], replicated, may hold values from 0 to 3, never falling along the last dimension, each value on 1 to 16 neighbouring positions
- doc_length: int32 [64, 4], replicated, may hold values from 20 to 180, as said below
Outputs:
- term_scores: float32 [256, 32000], P('voc', 'exp')
Inputs may be any that keep to these rules, and one draw needn't show every extreme that they name: `expert_routes`: each row names 2 different experts; among the rows of one exp index (32 tokens) no expert is named more than 16 times. `passage_ids`: never falling along a row; every passage holds 1 to 16 tokens. `doc_length`: positive whole numbers of words.
All inputs are finite; a program needn't handle non-finite values.
Results may differ from a plain program's by a relative error of at most 0.0065.
Values may be sent and summed in bfloat16 or wider, within the bound.
A program may use at most 128 MiB of HBM per device.

v0:
```python
import jax
import jax.numpy as jnp
from jax import lax
from jax.sharding import PartitionSpec as P

EXPERTS = 8


def slot_tables(route_rows, gate_rows, capacity):
    count = route_rows.shape[0]
    expert_ids = jnp.arange(EXPERTS, dtype=jnp.int32)
    hit_table = (route_rows[:, :, None] == expert_ids).astype(jnp.int32)
    flat_hits = hit_table.reshape(count * 2, EXPERTS)
    rank_table = jnp.cumsum(flat_hits, axis=0) - flat_hits
    slot_table = jnp.sum(flat_hits * rank_table, axis=1).reshape(count, 2)
    slot_ids = jnp.arange(capacity, dtype=jnp.int32)
    matches = hit_table[:, :, :, None] * (slot_table[:, :, None, None] == slot_ids).astype(
        jnp.int32
    )
    place_table = jnp.sum(matches, axis=1)
    gate_table = jnp.sum(matches.astype(jnp.float32) * gate_rows[:, :, None, None], axis=1)
    return (place_table, gate_table)


def build_slots(place_table, token_rows, group_size):
    slot_rows = jnp.einsum(
        "tec,td->ecd",
        place_table.astype(jnp.bfloat16),
        token_rows,
        preferred_element_type=jnp.float32,
    ).astype(jnp.bfloat16)
    return jnp.repeat(slot_rows, group_size, axis=0)


def local(
    tokens, expert_routes, gate_scores, w_gate, w_up, w_down, head_weight, passage_ids, doc_length
):
    tok_count, width_slice = tokens.shape
    capacity = tok_count // 2
    exp_count = lax.axis_size("exp")
    voc_count = lax.axis_size("voc")
    group_size = exp_count // EXPERTS
    place_table, gate_table = slot_tables(expert_routes, gate_scores, capacity)
    gate_local = w_gate[0]
    up_local = w_up[0]
    down_local = w_down[0]
    slot_count = exp_count * capacity
    send_rows = build_slots(place_table, tokens, group_size)
    received = lax.all_to_all(send_rows, "exp", split_axis=0, concat_axis=0, tiled=True)
    received = received.reshape(slot_count, width_slice)
    block_rows = lax.all_gather(received, "voc", axis=1, tiled=True)
    gate_pre = jnp.dot(block_rows, gate_local, preferred_element_type=jnp.float32)
    up_pre = jnp.dot(block_rows, up_local, preferred_element_type=jnp.float32)
    hidden = (jax.nn.silu(gate_pre) * up_pre).astype(jnp.bfloat16)
    part = jnp.dot(hidden, down_local, preferred_element_type=jnp.float32)
    rounded = lax.optimization_barrier(part.astype(jnp.bfloat16)).astype(jnp.float32)
    rounded = rounded.reshape(exp_count, capacity, rounded.shape[1])
    summed = lax.psum_scatter(rounded.astype(jnp.bfloat16), "voc", scatter_dimension=2, tiled=True)
    returned = lax.all_to_all(summed, "exp", split_axis=0, concat_axis=0, tiled=True)
    member_sum = jnp.sum(
        returned.astype(jnp.float32).reshape(EXPERTS, group_size, capacity, width_slice), axis=1
    )
    moe = jnp.einsum("tec,ecd->td", gate_table, member_sum, precision=lax.Precision.HIGHEST)
    layer_out = (tokens.astype(jnp.float32) + moe).astype(jnp.bfloat16)
    gathered = lax.all_gather(layer_out, "exp", axis=0, tiled=True)
    logits = lax.psum_scatter(
        jnp.dot(gathered, head_weight, preferred_element_type=jnp.float32).astype(jnp.bfloat16),
        "voc",
        scatter_dimension=0,
        tiled=True,
    ).astype(jnp.float32)
    saturated = jnp.log1p(jnp.maximum(logits, 0.0))
    shards_here = exp_count // voc_count
    pass_count = doc_length.shape[1]
    first_shard = lax.axis_index("voc") * shards_here
    ids_here = lax.dynamic_slice_in_dim(passage_ids, first_shard, shards_here, 0)
    lengths_here = lax.dynamic_slice_in_dim(doc_length, first_shard, shards_here, 0)
    one_hot = (
        ids_here[:, None, :] == jnp.arange(pass_count, dtype=jnp.int32)[None, :, None]
    ).astype(jnp.float32)
    saturated = saturated.reshape(shards_here, tok_count, saturated.shape[1])
    freq = jnp.einsum("spt,stv->spv", one_hot, saturated, precision=lax.Precision.HIGHEST)
    avg_length = jnp.sum(doc_length.astype(jnp.float32)) / (doc_length.shape[0] * pass_count)
    scale = 1.0 - 0.75 + 0.75 * lengths_here.astype(jnp.float32) / avg_length
    scores = freq * (1.2 + 1.0) / (freq + 1.2 * scale[:, :, None])
    return scores.reshape(shards_here * pass_count, scores.shape[2])


def solution(mesh):
    in_specs = (
        P("exp", "voc"),
        P("exp", None),
        P("exp", None),
        P("exp", None, "voc"),
        P("exp", None, "voc"),
        P("exp", "voc", None),
        P("voc", "exp"),
        P(),
        P(),
    )
    out_specs = P("voc", "exp")
    return jax.shard_map(local, mesh=mesh, in_specs=in_specs, out_specs=out_specs, check_vma=False)
```

profile of v0, /device:TPU:1, one launch (start us, length us, event | category | flops | bytes accessed | tf_op | source)
XLA Modules:
  0.0 445.1 jit_solution(3002805824108448492)
XLA Ops:
  6.5 0.8 copy.23
  7.4 0.7 fusion.20
  8.1 0.1 eq.65
  8.2 0.1 fusion.16
  8.2 0.1 reduce_window_sum.11
  8.3 0.2 select_reduce_fusion
  8.5 0.1 eq.69
  8.6 0.1 copy.24
  8.8 1.0 convolution_convert_fusion.2
  9.8 0.3 broadcast_in_dim.2
  10.1 62.7 %all_to_all.10 = bf16[64,16,1024]{2,1,0:T(8,128)(2,1)} all-to-all(bf16[64,16,1024]{2,1,0:T(8,128)(2,1)S(1)} %bitcast.38), channel_id=1, replica_groups=mesh['exp'=64,'voc'=4] {'exp'}, dimensions={0} | all-to-all | bytes 4194304 | tf_op jit(solution)/shard_map/all_to_all | solution.py:49
  72.9 83.4 %all-gather.3.cloned.1.call-done = bf16[1024,4096]{1,0:T(8,128)(2,1)} async-done(((bf16[1024,1024]{1,0:T(8,128)(2,1)}), bf16[1024,4096]{1,0:T(8,128)(2,1)}) %all-gather.3.cloned.1.call-update) | async-done | bytes 8388624 | tf_op jit(solution)/shard_map/all_gather | solution.py:51
  156.3 7.5 %fusion.3 = f32[1024,448]{0,1:T(8,128)S(1)} fusion(bf16[1024,4096]{1,0:T(8,128)(2,1)} %all-gather.3.cloned.1.call-done, bf16[1,4096,448]{1,2,0:T(8,128)(2,1)} %param.12), kind=kOutput, calls=%fused_computation.5 | convolution fusion | flops 3758096384 | bytes 13893632 | tf_op jit(solution)/shard_map/dot_general | solution.py:52
  163.8 15.2 %convolution_convert_fusion = bf16[1024,4096]{1,0:T(8,128)(2,1)} fusion(bf16[1,448,4096]{2,1,0:T(8,128)(2,1)} %param.14, f32[1024,448]{0,1:T(8,128)S(1)} %fusion.3, bf16[1024,4096]{1,0:T(8,128)(2,1)} %all-gather.3.cloned.1.call-done, bf16[1,4096,448]{1,2,0:T(8,128)(2,1)} %param.13), kind=kOutput, calls=%fused_computation | convolution fusion | flops 7523139584 | bytes 25952256 | tf_op jit(solution)/shard_map/dot_general | solution.py:55
  179.1 84.3 %reduce-scatter.3.cloned.1.call-done = bf16[64,16,1024]{2,1,0:T(8,128)(2,1)} async-done(((bf16[64,16,4096]{2,1,0:T(8,128)(2,1)}), bf16[64,16,1024]{2,1,0:T(8,128)(2,1)}) %reduce-scatter.3.cloned.1.call-update) | async-done | bytes 2097168 | tf_op jit(solution)/shard_map/reduce_scatter | solution.py:58
  263.4 10.6 %all-to-all-start.1 = ((bf16[64,16,1024]{2,1,0:T(8,128)(2,1)}), bf16[64,16,1024]{2,1,0:T(8,128)(2,1)S(1)}, u32[]{:S(2)}, u32[]{:S(2)}) async-start(bf16[64,16,1024]{2,1,0:T(8,128)(2,1)} %reduce-scatter.3.cloned.1.call-done), calls=%async_computation.2 | async-start | bytes 4194304 | tf_op jit(solution)/shard_map/all_to_all | solution.py:59
  274.1 49.6 %all-to-all-done.1 = bf16[64,16,1024]{2,1,0:T(8,128)(2,1)S(1)} async-done(((bf16[64,16,1024]{2,1,0:T(8,128)(2,1)}), bf16[64,16,1024]{2,1,0:T(8,128)(2,1)S(1)}, u32[]{:S(2)}, u32[]{:S(2)}) %all-to-all-start.1) | async-done | bytes 2097184 | tf_op jit(solution)/shard_map/all_to_all | solution.py:59
  323.7 0.4 convert_reduce_fusion
  324.0 1.0 fusion.10
  325.1 0.2 reduce-scatter.5.cloned.1.call-start
  325.4 75.4 %all-gather.5.cloned.1.call-done = bf16[2048,1024]{1,0:T(8,128)(2,1)} async-done(((bf16[32,1024]{1,0:T(8,128)(2,1)}), bf16[2048,1024]{1,0:T(8,128)(2,1)}) %all-gather.5.cloned.1.call-update) | async-done | bytes 4194320 | tf_op jit(solution)/shard_map/all_gather | solution.py:65
  400.8 5.8 %convolution_convert_fusion.1 = bf16[2048,500]{0,1:T(8,128)(2,1)} fusion(bf16[2048,1024]{1,0:T(8,128)(2,1)} %all-gather.5.cloned.1.call-done, bf16[1024,500]{0,1:T(8,128)(2,1)S(1)} %copy-done), kind=kOutput, calls=%fused_computation.7 | convolution fusion | flops 2098176000 | bytes 7266304 | tf_op jit(solution)/shard_map/dot_general | solution.py:67
  406.7 0.1 constant_dynamic-slice_fusion
  406.7 0.1 copy.22
  406.8 0.6 convert_reduce_fusion.1
  408.1 0.1 add_multiply_fusion
  408.2 0.1 copy.26
  408.2 27.4 %reduce-scatter.5.cloned.1.call-done = bf16[512,500]{0,1:T(8,128)(2,1)} async-done(((bf16[2048,500]{0,1:T(8,128)(2,1)}), bf16[512,500]{0,1:T(8,128)(2,1)}) %reduce-scatter.5.cloned.1.call-update) | async-done | bytes 512016 | tf_op jit(solution)/shard_map/reduce_scatter | solution.py:66
  435.6 1.4 maximum_log-plus-one_fusion
  437.1 0.3 copy.25
  437.4 0.5 add_divide_fusion
  437.9 0.7 reshape.46
  (20 shorter events, 0.2 us)
Async XLA Ops:
  6.5 394.3 %copy-start = (bf16[1024,500]{0,1:T(8,128)(2,1)S(1)}, bf16[1024,500]{0,1:T(8,128)(2,1)}, u32[]{:S(2)}) copy-start(bf16[1024,500]{0,1:T(8,128)(2,1)} %param.15) | copy-start | bytes 3072004
  6.5 149.7 %all-gather.3.cloned.1.call-start = ((), (), s32[]{:S(2)}) async-start(), calls=%async_computation.4 | async-start | bytes 10485760 | tf_op jit(solution)/shard_map/all_gather | solution.py:51
  72.8 190.5 %reduce-scatter.3.cloned.1.call-start = ((), (), s32[]{:S(2)}) async-start(), calls=%async_computation.5 | async-start | bytes 10485760 | tf_op jit(solution)/shard_map/reduce_scatter | solution.py:58
  179.1 95.0 %copy-start.4 = (f32[32,2]{0,1:T(2,128)S(1)}, f32[32,2]{0,1:T(2,128)}, u32[]{:S(2)}) copy-start(f32[32,2]{0,1:T(2,128)} %param.11) | copy-start | bytes 772
  179.1 144.9 %copy-start.1 = (bf16[32,1024]{1,0:T(8,128)(2,1)S(1)}, bf16[32,1024]{1,0:T(8,128)(2,1)}, u32[]{:S(2)}) copy-start(bf16[32,1024]{1,0:T(8,128)(2,1)} %param.9) | copy-start | bytes 196612
  263.4 60.3 %all-to-all-start.1 = ((bf16[64,16,1024]{2,1,0:T(8,128)(2,1)}), bf16[64,16,1024]{2,1,0:T(8,128)(2,1)S(1)}, u32[]{:S(2)}, u32[]{:S(2)}) async-start(bf16[64,16,1024]{2,1,0:T(8,128)(2,1)} %reduce-scatter.3.cloned.1.call-done), calls=%async_computation.2 | async-start | bytes 4194304 | tf_op jit(solution)/shard_map/all_to_all | solution.py:59
  274.0 126.8 %all-gather.5.cloned.1.call-start = ((), (), s32[]{:S(2)}) async-start(), calls=%async_computation.6 | async-start | bytes 4259840 | tf_op jit(solution)/shard_map/all_gather | solution.py:65
  325.1 81.6 %copy-start.2 = (s32[64,32]{0,1:T(8,128)S(1)}, s32[64,32]{0,1:T(8,128)}, u32[]{:S(2)}) copy-start(s32[64,32]{0,1:T(8,128)} %param.16) | copy-start | bytes 24580
  325.1 81.7 %copy-start.3 = (s32[64,4]{0,1:T(4,128)S(1)}, s32[64,4]{0,1:T(4,128)}, u32[]{:S(2)}) copy-start(s32[64,4]{0,1:T(4,128)} %param.17) | copy-start | bytes 3076
  325.1 110.5 %reduce-scatter.5.cloned.1.call-start = ((), (), s32[]{:S(2)}) async-start(), calls=%async_computation.7 | async-start | bytes 2580480 | tf_op jit(solution)/shard_map/reduce_scatter | solution.py:66
Sparse Core Ops, SparseCore 0:
  73.0 83.2 all-gather.2
  179.2 84.1 reduce-scatter.2
  325.2 75.5 all-gather.4
  406.8 28.8 reduce-scatter.4
where the time goes:
time: 445 us
  waiting for transfers between devices  320 us (72%)
  blocking collectives  62.7 us (14%)
  matrix products  31.2 us (7%)
  between operations  13.9 us (3%)
  starting transfers between devices  10.9 us (2%)
    reduce_scatter x1, waiting for transfers between devices, local(): lax.psum_scatter(rounded.astype(jnp.bfloat16), 'voc', scatter_dimension=2...  84.3 us
    all_gather x1, waiting for transfers between devices, local(): block_rows = lax.all_gather(received, 'voc', axis=1, tiled=True)  83.4 us
    all_gather x1, waiting for transfers between devices, local(): gathered = lax.all_gather(layer_out, 'exp', axis=0, tiled=True)  75.4 us
    all_to_all x1, blocking collectives, local(): lax.all_to_all(send_rows, 'exp', split_axis=0, concat_axis=0, tiled=True)  62.7 us
    all_to_all x1, waiting for transfers between devices, local(): lax.all_to_all(summed, 'exp', split_axis=0, concat_axis=0, tiled=True)  49.6 us
    reduce_scatter x1, waiting for transfers between devices, local(): lax.psum_scatter(jnp.dot(gathered, head_weight, preferred_element_type=jn...  27.4 us
    dot_general x1, matrix products, local(): part = jnp.dot(hidden, down_local, preferred_element_type=jnp.float32)  15.2 us
    all_to_all x1, starting transfers between devices, local(): lax.all_to_all(summed, 'exp', split_axis=0, concat_axis=0, tiled=True)  10.6 us
  transfers between devices with their start and end apart: 5, of which 5 were waited for; matrix products, arithmetic and copies ran while one was open for 0% of the time, Pallas kernels for 0%

commit v1 on v0

v1 whole, which is shorter than its diff:
```python
import jax
import jax.numpy as jnp
from jax import lax
from jax.experimental import pallas as pl
from jax.experimental.pallas import tpu as pltpu
from jax.sharding import PartitionSpec as P

MESH = pl.DeviceIdType.MESH
BF16, F32 = jnp.bfloat16, jnp.float32
EXPERTS = 8
CAP = 16
TOK = 32
WIDTH = 1024
FEATURES = 4096
CHUNKS = 4
PASSAGES_HERE = 64
SENDS = 320
NT = (((1,), (1,)), ((), ()))


def aligned(value, step):
    return pl.multiple_of(value, step)


def kernel(
    tok, routes, gates, w_gate, w_up, w_down, head, ids, lengths, out,
    X, PART, PREC, S, RA, RB, TA, TB, RA2, RB2, U, RET, SLOT, WG, WU, WD, HW, LG, LS, LR,
    send_sem, recv_sem, local_sem,
):
    index = lax.axis_index("exp")
    x = lax.axis_index("voc")
    z, y, c = index // 8, (index // 2) % 4, index % 2

    def at(dx=0, dy=0, dz=0, dc=0):
        return (((z + dz) % 8) * 8 + ((y + dy) % 4) * 2 + (c + dc) % 2, (x + dx) % 4)

    weights = [
        pltpu.make_async_copy(src, dst, local_sem.at[i])
        for i, (src, dst) in enumerate([(w_gate, WG), (w_up, WU), (w_down, WD), (head, HW)])
    ]
    for copy in weights:
        copy.start()

    partners = (
        [at(dx=i) for i in (1, 2, 3)]
        + [at(dy=i) for i in (1, 2, 3)]
        + [at(dz=i) for i in range(1, 8)]
        + [at(dc=1)]
    )
    barrier = pltpu.get_barrier_semaphore()
    for partner in partners:
        pl.semaphore_signal(barrier, inc=1, device_id=partner, device_id_type=MESH)

    slot_row = lax.broadcasted_iota(jnp.int32, (EXPERTS * CAP, TOK), 0)
    expert_of, slot_of = slot_row // CAP, slot_row % CAP
    first, second = routes[0:1, :] == expert_of, routes[1:2, :] == expert_of
    hit = (first | second).astype(F32)
    earlier = (
        lax.broadcasted_iota(jnp.int32, (TOK, TOK), 0)
        < lax.broadcasted_iota(jnp.int32, (TOK, TOK), 1)
    ).astype(F32)
    rank = jnp.dot(hit.astype(BF16), earlier.astype(BF16), preferred_element_type=F32)
    place = jnp.where(rank == slot_of.astype(F32), hit, 0.0)
    SLOT[...] = jnp.dot(place.astype(BF16), tok[...], preferred_element_type=F32).astype(BF16)
    gate_of = place * (jnp.where(first, gates[0:1, :], 0.0) + jnp.where(second, gates[1:2, :], 0.0))

    pl.semaphore_wait(barrier, len(partners))

    copies = []

    def send(src, dst, target):
        n = len(copies)
        copy = pltpu.make_async_remote_copy(
            src_ref=src, dst_ref=dst, send_sem=send_sem.at[n], recv_sem=recv_sem.at[n],
            device_id=target, device_id_type=MESH,
        )
        copy.start()
        copies.append(copy)
        return copy

    def arrived(group):
        for copy in group:
            copy.wait_recv()

    my_cols = pl.ds(aligned(x * WIDTH, WIDTH), WIDTH)

    def cols(i):
        return pl.ds(aligned(((x + i) % 4) * WIDTH, WIDTH), WIDTH)

    def rows(k, u, core, yy, count):
        return pl.ds(aligned(((k * 2 + u) * 2 + core) * 64 + yy * CAP, CAP), count)

    def block(k, u):
        return X.at[rows(k, u, c, y, CAP), my_cols]

    from_z = {}
    for k in range(CHUNKS):
        for u, d in ((0, k), (1, 7 - k)):
            if d == 0:
                X[rows(k, u, c, y, CAP), my_cols] = SLOT[pl.ds(aligned(z * CAP, CAP), CAP), :]
                from_z[k, u] = []
            else:
                src = SLOT.at[pl.ds(aligned(((z + d) % 8) * CAP, CAP), CAP), :]
                from_z[k, u] = [send(src, block(k, u), at(dz=d))]

    a1, a2, a3, d1, r1, r2, r3 = {}, {}, {}, {}, {}, {}, {}

    def gather_first(k):
        arrived(from_z[k, 0])
        a1[k] = [send(block(k, 0), block(k, 0), at(dx=i)) for i in (2, 1, 3)]
        arrived(from_z[k, 1])
        a1[k] += [send(block(k, 1), block(k, 1), at(dy=i)) for i in (2, 1, 3)]

    def gather_second(k):
        arrived(a1[k])
        ours = X.at[rows(k, 0, c, y, CAP), :]
        a2[k] = [send(ours, ours, at(dy=i)) for i in (2, 1, 3)]
        ours = X.at[rows(k, 1, c, 0, 64), my_cols]
        a2[k] += [send(ours, ours, at(dx=i)) for i in (2, 1, 3)]

    def gather_cores(k):
        arrived(a2[k])
        a3[k] = []
        for u in (0, 1):
            ours = X.at[rows(k, u, c, 0, 64), :]
            a3[k].append(send(ours, ours, at(dc=1)))

    hidden = {}

    def gate_up(k):
        arrived(a3[k])
        here = X[k * 256 : (k + 1) * 256, :]
        gate_pre = lax.dot_general(here, WG[...], NT, preferred_element_type=F32)
        up_pre = lax.dot_general(here, WU[...], NT, preferred_element_type=F32)
        hidden[k] = (gate_pre / (1.0 + jnp.exp(-gate_pre)) * up_pre).astype(BF16)

    def down(k):
        for n in range(4):
            part = slice(n * WIDTH, (n + 1) * WIDTH)
            PART[k * 256 : (k + 1) * 256, part] = jnp.dot(
                hidden[k], WD[:, part], preferred_element_type=F32
            ).astype(BF16)
        d1[k] = [
            send(PART.at[rows(k, u, 1 - c, 0, 64), :], PREC.at[pl.ds((k * 2 + u) * 64, 64), :], at(dc=1))
            for u in (0, 1)
        ]

    def reduce_first(k):
        arrived(d1[k])
        for u in (0, 1):
            to = pl.ds((k * 2 + u) * 64, 64)
            S[to, :] = (
                PART[rows(k, u, c, 0, 64), :].astype(F32) + PREC[to, :].astype(F32)
            ).astype(BF16)
        r1[k] = []
        for i in (2, 1, 3):
            src = S.at[pl.ds(aligned(k * 128 + ((y + i) % 4) * CAP, CAP), CAP), :]
            r1[k].append(send(src, RA.at[k, i - 1], at(dy=i)))
            src = S.at[pl.ds(k * 128 + 64, 64), cols(i)]
            r1[k].append(send(src, RB.at[k, i - 1], at(dx=i)))

    def reduce_second(k):
        arrived(r1[k])
        total = S[pl.ds(aligned(k * 128 + y * CAP, CAP), CAP), :].astype(F32)
        for i in range(3):
            total = total + RA[k, i].astype(F32)
        TA[k] = total.astype(BF16)
        total = S[k * 128 + 64 : k * 128 + 128, my_cols].astype(F32)
        for i in range(3):
            total = total + RB[k, i].astype(F32)
        TB[k] = total.astype(BF16)
        r2[k] = []
        for i in (2, 1, 3):
            r2[k].append(send(TA.at[k, :, cols(i)], RA2.at[k, i - 1], at(dx=i)))
            src = TB.at[k, pl.ds(aligned(((y + i) % 4) * CAP, CAP), CAP), :]
            r2[k].append(send(src, RB2.at[k, i - 1], at(dy=i)))

    mine = pl.ds(aligned(z * CAP, CAP), CAP)

    def give_back(k):
        arrived(r2[k])
        r3[k] = []
        for u, (own, more) in enumerate(
            [
                (TA[k, :, my_cols], RA2),
                (TB[k, pl.ds(aligned(y * CAP, CAP), CAP), :], RB2),
            ]
        ):
            total = own.astype(F32)
            for i in range(3):
                total = total + more[k, i].astype(F32)
            if u == 0 and k == 0:
                RET[mine, :] = total.astype(BF16)
            else:
                U[k, u] = total.astype(BF16)
                dz = -k if u == 0 else 1 + k
                r3[k].append(send(U.at[k, u], RET.at[mine, :], at(dz=dz % 8)))

    gather_first(0)
    gather_first(1)
    gather_second(0)
    gather_first(2)
    gather_second(1)
    gather_first(3)
    gather_cores(0)
    gather_second(2)
    for copy in weights[:3]:
        copy.wait()
    gate_up(0)
    gather_cores(1)
    gather_second(3)
    down(0)
    gate_up(1)
    reduce_first(0)
    gather_cores(2)
    down(1)
    gate_up(2)
    reduce_first(1)
    gather_cores(3)
    reduce_second(0)
    down(2)
    gate_up(3)
    reduce_first(2)
    give_back(0)
    reduce_second(1)
    down(3)
    give_back(1)
    reduce_second(2)
    reduce_first(3)
    give_back(2)
    reduce_second(3)
    give_back(3)

    eye = (
        lax.broadcasted_iota(jnp.int32, (TOK, TOK), 0)
        == lax.broadcasted_iota(jnp.int32, (TOK, TOK), 1)
    ).astype(F32)
    highest = lax.Precision.HIGHEST
    gate_table = lax.dot_general(eye, gate_of, NT, precision=highest, preferred_element_type=F32)
    for k in range(CHUNKS):
        arrived(r3[k])
    moe = jnp.dot(gate_table, RET[...].astype(F32), precision=highest, preferred_element_type=F32)
    LG[z, y, c] = (tok[...].astype(F32) + moe).astype(BF16)

    ours = LG.at[z, y, c]
    to_planes = [send(ours, ours, at(dz=d)) for d in (4, 3, 5, 2, 6, 1, 7)]

    passage = lax.broadcasted_iota(jnp.int32, (PASSAGES_HERE, 64), 0)
    pick = (lax.broadcasted_iota(jnp.int32, (PASSAGES_HERE, 64), 1) == passage // 4 + 16 * x).astype(F32)
    ids_of = lax.dot_general(pick, ids[...].astype(F32), NT, precision=highest, preferred_element_type=F32)
    spread = (
        lax.broadcasted_iota(jnp.int32, (TOK, 512), 1) % TOK
        == lax.broadcasted_iota(jnp.int32, (TOK, 512), 0)
    ).astype(F32)
    ids_of = jnp.dot(ids_of, spread, precision=highest, preferred_element_type=F32)
    passage = lax.broadcasted_iota(jnp.int32, (PASSAGES_HERE, 512), 0)
    token = lax.broadcasted_iota(jnp.int32, (PASSAGES_HERE, 512), 1)
    one_hot = ((ids_of == (passage % 4).astype(F32)) & (token // TOK == passage // 4)).astype(F32)
    words = lengths[...].astype(F32)
    average = jnp.sum(words) / 256.0
    words = lax.dot_general(pick, words, NT, precision=highest, preferred_element_type=F32)
    passage = lax.broadcasted_iota(jnp.int32, (PASSAGES_HERE, 4), 0)
    which = lax.broadcasted_iota(jnp.int32, (PASSAGES_HERE, 4), 1)
    words = jnp.sum(jnp.where(which == passage % 4, words, 0.0), axis=1, keepdims=True)
    scale = 1.0 - 0.75 + 0.75 * words / average

    weights[3].wait()
    arrived(to_planes)
    h1, h2, h3 = {}, {}, []

    def pair(i):
        return pl.ds(((x + 1 + i) % 4) * 2, 2)

    def spread_first(i):
        block = LG.at[pair(i), y, c]
        h1[i] = [send(block, block, at(dy=n)) for n in (2, 1, 3)]

    def spread_cores(i):
        arrived(h1[i])
        block = LG.at[pair(i), :, c]
        h2[i] = [send(block, block, at(dc=1))]

    def logits(i):
        arrived(h2[i])
        here = LG[pair(i)].reshape(512, WIDTH)
        return lax.dot_general(here, HW[...], NT, preferred_element_type=F32)

    def head_part(i):
        LS[i] = logits(i).astype(BF16)
        h3.append(send(LS.at[i], LR.at[i], at(dx=1 + i)))

    spread_first(0)
    spread_first(1)
    spread_cores(0)
    spread_first(2)
    head_part(0)
    spread_cores(1)
    spread_first(3)
    head_part(1)
    spread_cores(2)
    head_part(2)
    spread_cores(3)
    total = logits(3)
    arrived(h3)
    for i in range(3):
        total = total + LR[i].astype(F32)
    saturated = jnp.log1p(jnp.maximum(total, 0.0))
    freq = jnp.dot(one_hot, saturated, precision=highest, preferred_element_type=F32)
    out[...] = freq * (1.2 + 1.0) / (freq + 1.2 * scale)

    for copy in copies:
        copy.wait_send()


def local(
    tokens, expert_routes, gate_scores, w_gate, w_up, w_down, head_weight, passage_ids, doc_length
):
    vmem, anywhere = pl.BlockSpec(memory_space=pltpu.VMEM), pl.BlockSpec(memory_space=pl.ANY)
    hidden_units, terms = w_gate.shape[2], head_weight.shape[1]

    def buffer(*shape):
        return pltpu.VMEM(shape, BF16)

    return pl.pallas_call(
        kernel,
        out_shape=jax.ShapeDtypeStruct((PASSAGES_HERE, terms), F32),
        in_specs=[vmem] * 3 + [anywhere] * 4 + [vmem] * 2,
        out_specs=vmem,
        scratch_shapes=[
            buffer(1024, FEATURES),
            buffer(1024, FEATURES),
            buffer(512, FEATURES),
            buffer(512, FEATURES),
            buffer(CHUNKS, 3, CAP, FEATURES),
            buffer(CHUNKS, 3, 64, WIDTH),
            buffer(CHUNKS, CAP, FEATURES),
            buffer(CHUNKS, 64, WIDTH),
            buffer(CHUNKS, 3, CAP, WIDTH),
            buffer(CHUNKS, 3, CAP, WIDTH),
            buffer(CHUNKS, 2, CAP, WIDTH),
            buffer(EXPERTS * CAP, WIDTH),
            buffer(EXPERTS * CAP, WIDTH),
            buffer(hidden_units, FEATURES),
            buffer(hidden_units, FEATURES),
            buffer(hidden_units, FEATURES),
            buffer(terms, WIDTH),
            buffer(8, 4, 2, TOK, WIDTH),
            buffer(3, 512, terms),
            buffer(3, 512, terms),
            pltpu.SemaphoreType.DMA((SENDS,)),
            pltpu.SemaphoreType.DMA((SENDS,)),
            pltpu.SemaphoreType.DMA((4,)),
        ],
        compiler_params=pltpu.CompilerParams(
            collective_id=0, has_side_effects=True, vmem_limit_bytes=60 * 2**20
        ),
        cost_estimate=pl.CostEstimate(
            flops=14_000_000_000, bytes_accessed=13_000_000, transcendentals=800_000
        ),
    )(
        tokens,
        expert_routes.T,
        gate_scores.T,
        w_gate[0].T,
        w_up[0].T,
        w_down[0],
        head_weight.T,
        passage_ids.T,
        doc_length.T,
    )


def solution(mesh):
    in_specs = (
        P("exp", "voc"),
        P("exp", None),
        P("exp", None),
        P("exp", None, "voc"),
        P("exp", None, "voc"),
        P("exp", "voc", None),
        P("voc", "exp"),
        P(),
        P(),
    )
    return jax.shard_map(
        local, mesh=mesh, in_specs=in_specs, out_specs=P("voc", "exp"), check_vma=False
    )
```

time: 445 us -> 149 us (0.33)
  waiting for transfers between devices: 320 us -> 0 us
  Pallas kernels: 0 us -> 147 us
  blocking collectives: 62.7 us -> 0 us
  matrix products: 31.2 us -> 0 us
  between operations: 13.9 us -> 0.01 us
  starting transfers between devices: 10.9 us -> 0 us
    all_gather x2 -> x0, waiting for transfers between devices: 159 us -> none  [the longest x1 83.4 us: local(): block_rows = lax.all_gather(received, 'voc', axis=1, tiled=True)]
    pallas_call x0 -> x1, Pallas kernels: none -> 147 us  [local(): pl.pallas_call(kernel, out_shape=jax.ShapeDtypeStruct((PASSAGES_HERE, ter...]
    reduce_scatter x2 -> x0, waiting for transfers between devices: 112 us -> none  [the longest x1 84.3 us: local(): lax.psum_scatter(rounded.astype(jnp.bfloat16), 'voc', scatter_dimension=2...]
    all_to_all x1 -> x0, blocking collectives: 62.7 us -> none  [local(): lax.all_to_all(send_rows, 'exp', split_axis=0, concat_axis=0, tiled=True)]
    all_to_all x1 -> x0, waiting for transfers between devices: 49.6 us -> none  [local(): lax.all_to_all(summed, 'exp', split_axis=0, concat_axis=0, tiled=True)]
    dot_general x6 -> x0, matrix products: 31.2 us -> none  [the longest x1 15.2 us: local(): part = jnp.dot(hidden, down_local, preferred_element_type=jnp.float32)]
    all_to_all x1 -> x0, starting transfers between devices: 10.6 us -> none  [local(): lax.all_to_all(summed, 'exp', split_axis=0, concat_axis=0, tiled=True)]
  transfers between devices with their start and end apart: 5 -> 0, of which waited for: 5 -> 0; matrix products, arithmetic and copies ran while one was open for 0% -> 0% of each run, Pallas kernels for 0% -> 0%
where the time goes in v1:
time: 149 us
  Pallas kernels  147 us (99%)
  local copies, waits for them, and re-layouts  1.57 us (1%)
    pallas_call x1, Pallas kernels, local(): pl.pallas_call(kernel, out_shape=jax.ShapeDtypeStruct((PASSAGES_HERE, ter...  147 us

profile of v1, /device:TPU:1, one launch (start us, length us, event | category | flops | bytes accessed | tf_op | source)
XLA Modules:
  0.0 149.0 jit_solution(14012746461880948369)
XLA Ops:
  0.0 147.4 %shard_map.91 = f32[64,500]{1,0:T(8,128)} custom-call(bf16[32,1024]{1,0:T(8,128)(2,1)} %tok.1, s32[2,32]{1,0:T(2,128)} %bitcast.18, f32[2,32]{1,0:T(2,128)} %bitcast.19, bf16[448,4096]{1,0:T(8,128)(2,1)} %bitcast.12, bf16[448,4096]{1,0:T(8,128)(2,1)} %bitcast.13, bf16[448,4096]{1,0:T(8,128)(2,1)} %bitcast.14, bf16[500,1024]{1,0:T(8,128)(2,1)} %bitcast.15, ...), custom_call_target="tpu_custom_call" | custom-call | flops 14000000000 | bytes 13000000 | tf_op jit(solution)/shard_map/pallas_call | solution.py:324
  147.4 1.6 %copy.11 = f32[64,500]{1,0:T(8,128)} copy(f32[64,500]{1,0:T(8,128)} %shard_map.91) | data formatting | bytes 256000

commit v2 on v1

v2 whole, which is shorter than its diff:
```python
import math

import jax
import jax.numpy as jnp
from jax import lax
from jax.experimental import pallas as pl
from jax.experimental.pallas import tpu as pltpu
from jax.sharding import PartitionSpec as P

MESH = pl.DeviceIdType.MESH
BF16, F32 = jnp.bfloat16, jnp.float32
EXPERTS = 8
CAP = 16
TOK = 32
WIDTH = 1024
FEATURES = 4096
CHUNKS = 4
PASSAGES_HERE = 64
SEND_SEMS = 22
RECV_SEMS = 66
NT = (((1,), (1,)), ((), ()))


def aligned(value, step):
    return pl.multiple_of(value, step)


def kernel(
    tok, routes, gates, w_gate, w_up, w_down, head, ids, lengths, out,
    X, PART, PREC, S, QA, VA, RA, QB, VB, RB, TA, TB, RA2, RB2, U, RET, SLOT, WG, WU, WD, HW,
    LG, LS, QX, RX, FS, FR, send_sem, recv_sem, local_sem,
):
    index = lax.axis_index("exp")
    x = lax.axis_index("voc")
    z, y, c = index // 8, (index // 2) % 4, index % 2
    odd = z % 2

    def at(dx=0, dy=0, dz=0, dc=0):
        return (((z + dz + 8) % 8) * 8 + ((y + dy) % 4) * 2 + (c + dc) % 2, (x + dx) % 4)

    weights = [
        pltpu.make_async_copy(src, dst, local_sem.at[i])
        for i, (src, dst) in enumerate([(head, HW.at[odd]), (w_gate, WG), (w_up, WU), (w_down, WD)])
    ]
    for copy in weights:
        copy.start()

    partners = (
        [at(dx=i) for i in (1, 2, 3)]
        + [at(dy=i) for i in (1, 2, 3)]
        + [at(dz=i) for i in range(1, 8)]
        + [at(dc=1)]
    )
    barrier = pltpu.get_barrier_semaphore()
    for partner in partners:
        pl.semaphore_signal(barrier, inc=1, device_id=partner, device_id_type=MESH)

    slot_row = lax.broadcasted_iota(jnp.int32, (EXPERTS * CAP, TOK), 0)
    expert_of, slot_of = slot_row // CAP, slot_row % CAP
    first, second = routes[0:1, :] == expert_of, routes[1:2, :] == expert_of
    hit = (first | second).astype(F32)
    earlier = (
        lax.broadcasted_iota(jnp.int32, (TOK, TOK), 0)
        < lax.broadcasted_iota(jnp.int32, (TOK, TOK), 1)
    ).astype(F32)
    rank = jnp.dot(hit.astype(BF16), earlier.astype(BF16), preferred_element_type=F32)
    place = jnp.where(rank == slot_of.astype(F32), hit, 0.0)
    SLOT[...] = jnp.dot(place.astype(BF16), tok[...], preferred_element_type=F32).astype(BF16)
    gate_of = place * (jnp.where(first, gates[0:1, :], 0.0) + jnp.where(second, gates[1:2, :], 0.0))

    pl.semaphore_wait(barrier, len(partners))

    kinds, stages, singles = {}, [], []
    used = [0, 0]

    def fresh(which):
        used[which] += 1
        return used[which] - 1

    def sized(units):
        if units <= 8:
            return SLOT.at[pl.ds(0, units * 16), :]
        assert units % 4 == 0
        return X.at[pl.ds(0, units * 4), :]

    def remote(src, dst, send_n, recv_n, target):
        return pltpu.make_async_remote_copy(
            src_ref=src, dst_ref=dst, send_sem=send_sem.at[send_n], recv_sem=recv_sem.at[recv_n],
            device_id=target, device_id_type=MESH,
        )

    def stage(kind, moves):
        if kind not in kinds:
            kinds[kind] = [fresh(0), 0]
        recv_n, units = fresh(1), 0
        for src, dst, target in moves:
            remote(src, dst, kinds[kind][0], recv_n, target).start()
            units += math.prod(src.shape) // (16 * WIDTH)
        kinds[kind][1] += units
        return (kinds[kind][0], recv_n, units)

    def arrived(done):
        send_n, recv_n, units = done
        remote(sized(units), sized(units), send_n, recv_n, at(dc=1)).wait_recv()

    def send(src, dst, target):
        copy = remote(src, dst, fresh(0), fresh(1), target)
        copy.start()
        singles.append(copy)
        return copy

    def span(start, step, size=None):
        return pl.ds(aligned(start, step), size or step)

    my_cols = span(x * WIDTH, WIDTH)

    def cols(i):
        return span(((x + i) % 4) * WIDTH, WIDTH)

    def half_cols(i, half):
        return span(((x + i) % 4) * WIDTH + half * 512, 512)

    def rows(k, u, core, yy, count):
        return pl.ds(aligned(((k * 2 + u) * 2 + core) * 64 + (yy % 4) * CAP, CAP), count)

    halves = (pl.ds(0, 2048), pl.ds(2048, 2048))

    def block(k, u):
        return X.at[rows(k, u, c, y, CAP), my_cols]

    from_z = {}
    for k in range(CHUNKS):
        for u, d in ((0, k), (1, 7 - k)):
            if d == 0:
                X[rows(k, u, c, y, CAP), my_cols] = SLOT[span(z * CAP, CAP), :]
            else:
                src = SLOT.at[span(((z + d) % 8) * CAP, CAP), :]
                from_z[k, u] = stage("z", [(src, block(k, u), at(dz=d))])

    a1, a2, ar, a3, d1, r1, rd, rr, r2, r3 = {}, {}, {}, {}, {}, {}, {}, {}, {}, {}

    def gather_first(k):
        if k:
            arrived(from_z[k, 0])
        arrived(from_z[k, 1])
        here, there = block(k, 0), block(k, 1)
        moves = [(here, here, at(dx=i)) for i in (2, 1, 3)]
        a1[k] = stage("a1", moves + [(there, there, at(dy=i)) for i in (2, 1, 3)])

    def gather_second(k):
        arrived(a1[k])
        here, there = X.at[rows(k, 0, c, y, CAP), :], X.at[rows(k, 1, c, 0, 64), my_cols]
        moves = [(here, here, at(dy=i)) for i in (1, 3)]
        a2[k] = stage("a2", moves + [(there, there, at(dx=i)) for i in (1, 3)])

    def gather_relay(k):
        arrived(a2[k])
        moves = []
        for half, (came, goes) in enumerate(((3, 1), (1, 3))):
            block = X.at[rows(k, 0, c, y + came, CAP), halves[half]]
            moves.append((block, block, at(dy=goes)))
            block = X.at[rows(k, 1, c, 0, 64), half_cols(came, half)]
            moves.append((block, block, at(dx=goes)))
        ar[k] = stage("ar", moves)

    def gather_cores(k):
        arrived(ar[k])
        blocks = [X.at[rows(k, u, c, 0, 64), :] for u in (0, 1)]
        a3[k] = stage("a3", [(block, block, at(dc=1)) for block in blocks])

    hidden = {}

    def gate_up(k):
        arrived(a3[k])
        here = X[k * 256 : (k + 1) * 256, :]
        gate_pre = lax.dot_general(here, WG[...], NT, preferred_element_type=F32)
        up_pre = lax.dot_general(here, WU[...], NT, preferred_element_type=F32)
        hidden[k] = (gate_pre / (1.0 + jnp.exp(-gate_pre)) * up_pre).astype(BF16)

    def down(k):
        for n in range(4):
            part = slice(n * WIDTH, (n + 1) * WIDTH)
            PART[k * 256 : (k + 1) * 256, part] = jnp.dot(
                hidden[k], WD[:, part], preferred_element_type=F32
            ).astype(BF16)
        d1[k] = stage("d1", [
            (PART.at[rows(k, u, 1 - c, 0, 64), :], PREC.at[pl.ds((k * 2 + u) * 64, 64), :], at(dc=1))
            for u in (0, 1)
        ])

    def s_rows(k, i):
        return span(k * 128 + ((y + i) % 4) * CAP, CAP)

    def reduce_first(k):
        arrived(d1[k])
        for u in (0, 1):
            to = pl.ds((k * 2 + u) * 64, 64)
            S[to, :] = (
                PART[rows(k, u, c, 0, 64), :].astype(F32) + PREC[to, :].astype(F32)
            ).astype(BF16)
        s64 = pl.ds(k * 128 + 64, 64)
        moves, direct = [], []
        for half, goes in enumerate((1, 3)):
            moves.append((S.at[s_rows(k, 2), halves[half]], QA.at[k, half], at(dy=goes)))
            moves.append((S.at[s64, half_cols(2, half)], QB.at[k, half], at(dx=goes)))
            more = 1 - half
            dst = RA.at[k, half, :, halves[more]]
            direct.append((S.at[s_rows(k, goes), halves[more]], dst, at(dy=goes)))
            dst = RB.at[k, half, :, pl.ds(more * 512, 512)]
            direct.append((S.at[s64, half_cols(goes, more)], dst, at(dx=goes)))
        r1[k] = stage("r1", moves)
        rd[k] = stage("rd", direct)

    def reduce_relay(k):
        arrived(r1[k])
        s64 = pl.ds(k * 128 + 64, 64)
        moves = []
        for half, goes in enumerate((1, 3)):
            VA[k, half] = (
                S[s_rows(k, goes), halves[half]].astype(F32) + QA[k, half].astype(F32)
            ).astype(BF16)
            moves.append((VA.at[k, half], RA.at[k, half, :, halves[half]], at(dy=goes)))
            VB[k, half] = (
                S[s64, half_cols(goes, half)].astype(F32) + QB[k, half].astype(F32)
            ).astype(BF16)
            moves.append((VB.at[k, half], RB.at[k, half, :, pl.ds(half * 512, 512)], at(dx=goes)))
        rr[k] = stage("rr", moves)

    def reduce_second(k):
        arrived(rd[k])
        arrived(rr[k])
        total = S[s_rows(k, 0), :].astype(F32)
        TA[k] = (total + RA[k, 0].astype(F32) + RA[k, 1].astype(F32)).astype(BF16)
        total = S[k * 128 + 64 : k * 128 + 128, my_cols].astype(F32)
        TB[k] = (total + RB[k, 0].astype(F32) + RB[k, 1].astype(F32)).astype(BF16)
        moves = []
        for i in (2, 1, 3):
            moves.append((TA.at[k, :, cols(i)], RA2.at[k, i - 1], at(dx=i)))
            src = TB.at[k, span(((y + i) % 4) * CAP, CAP), :]
            moves.append((src, RB2.at[k, i - 1], at(dy=i)))
        r2[k] = stage("r2", moves)

    mine = span(z * CAP, CAP)

    def give_back(k):
        arrived(r2[k])
        moves = []
        for u, (own, more) in enumerate(
            [(TA[k, :, my_cols], RA2), (TB[k, span(y * CAP, CAP), :], RB2)]
        ):
            total = own.astype(F32)
            for i in range(3):
                total = total + more[k, i].astype(F32)
            if u == 0 and k == 0:
                RET[mine, :] = total.astype(BF16)
            else:
                U[k, u] = total.astype(BF16)
                moves.append((U.at[k, u], RET.at[mine, :], at(dz=-k if u == 0 else 1 + k)))
        r3[k] = stage("r3", moves)

    gather_first(0)
    gather_first(1)
    gather_second(0)
    gather_first(2)
    gather_second(1)
    gather_first(3)
    gather_relay(0)
    gather_second(2)
    weights[0].wait()
    swap = at(dz=1 - 2 * odd)
    head_copy = send(HW.at[odd], HW.at[odd], swap)
    gather_cores(0)
    gather_relay(1)
    gather_second(3)
    for copy in weights[1:]:
        copy.wait()
    gate_up(0)
    gather_cores(1)
    gather_relay(2)
    down(0)
    gate_up(1)
    gather_cores(2)
    gather_relay(3)
    reduce_first(0)
    down(1)
    gate_up(2)
    gather_cores(3)
    reduce_first(1)
    reduce_relay(0)
    down(2)
    gate_up(3)
    reduce_first(2)
    reduce_second(0)
    reduce_relay(1)
    down(3)
    reduce_second(1)
    reduce_relay(2)
    give_back(0)
    reduce_first(3)
    give_back(1)
    reduce_second(2)
    reduce_relay(3)
    give_back(2)
    reduce_second(3)
    give_back(3)

    eye = (
        lax.broadcasted_iota(jnp.int32, (TOK, TOK), 0)
        == lax.broadcasted_iota(jnp.int32, (TOK, TOK), 1)
    ).astype(F32)
    highest = lax.Precision.HIGHEST
    gate_table = lax.dot_general(eye, gate_of, NT, precision=highest, preferred_element_type=F32)
    for k in range(CHUNKS):
        arrived(r3[k])
    moe = jnp.dot(gate_table, RET[...].astype(F32), precision=highest, preferred_element_type=F32)
    LG[z // 2, y, c] = (tok[...].astype(F32) + moe).astype(BF16)

    ours = LG.at[z // 2, y, c]
    to_planes = stage("l0", [(ours, ours, at(dz=d)) for d in (4, 2, 6)])

    def picks(count, first_shard):
        passage = lax.broadcasted_iota(jnp.int32, (count, 64), 0)
        shard = lax.broadcasted_iota(jnp.int32, (count, 64), 1)
        return (shard == passage // 4 + first_shard).astype(F32)

    ids_of = lax.dot_general(
        picks(32, 16 * x + 8 * odd), ids[...].astype(F32), NT,
        precision=highest, preferred_element_type=F32,
    )
    spread = (
        lax.broadcasted_iota(jnp.int32, (TOK, 256), 1) % TOK
        == lax.broadcasted_iota(jnp.int32, (TOK, 256), 0)
    ).astype(F32)
    ids_of = jnp.dot(ids_of, spread, precision=highest, preferred_element_type=F32)
    passage = lax.broadcasted_iota(jnp.int32, (32, 256), 0)
    token = lax.broadcasted_iota(jnp.int32, (32, 256), 1)
    one_hot = ((ids_of == (passage % 4).astype(F32)) & (token // TOK == passage // 4)).astype(F32)
    words = lengths[...].astype(F32)
    average = jnp.sum(words) / 256.0
    words = lax.dot_general(
        picks(PASSAGES_HERE, 16 * x), words, NT, precision=highest, preferred_element_type=F32
    )
    passage = lax.broadcasted_iota(jnp.int32, (PASSAGES_HERE, 4), 0)
    which = lax.broadcasted_iota(jnp.int32, (PASSAGES_HERE, 4), 1)
    words = jnp.sum(jnp.where(which == passage % 4, words, 0.0), axis=1, keepdims=True)
    scale = 1.0 - 0.75 + 0.75 * words / average

    head_copy.wait_recv()
    arrived(to_planes)
    h1, h2 = {}, {}

    def spread_first(i):
        block = LG.at[(x + i) % 4, y, c]
        h1[i] = stage("h1", [(block, block, at(dy=n)) for n in (2, 1, 3)])

    def spread_cores(i):
        arrived(h1[i])
        block = LG.at[(x + i) % 4, :, c]
        h2[i] = stage("h2", [(block, block, at(dc=1))])

    def logits(i):
        arrived(h2[i])
        here = LG[(x + i) % 4].reshape(256, WIDTH)
        return [lax.dot_general(here, HW[v], NT, preferred_element_type=F32) for v in (0, 1)]

    spread_first(2)
    spread_first(1)
    spread_cores(2)
    spread_first(3)
    part = logits(2)
    halfway = []
    for v, goes in enumerate((1, 3)):
        LS[0, v] = part[v].astype(BF16)
        halfway.append(send(LS.at[0, v], QX.at[v], at(dx=goes)))
    spread_cores(1)
    spread_first(0)
    part = logits(1)
    last = []
    LS[1, 1] = part[1].astype(BF16)
    last.append(send(LS.at[1, 1], RX.at[0, 1], at(dx=1)))
    LS[1, 0] = part[0].astype(BF16)
    spread_cores(3)
    part = logits(3)
    LS[2, 0] = part[0].astype(BF16)
    last.append(send(LS.at[2, 0], RX.at[1, 0], at(dx=3)))
    LS[2, 1] = part[1].astype(BF16)
    for v, goes in enumerate((1, 3)):
        halfway[v].wait_recv()
        LS[1 + v, v] = (LS[1 + v, v].astype(F32) + QX[v].astype(F32)).astype(BF16)
        last.append(send(LS.at[1 + v, v], RX.at[v, v], at(dx=goes)))
    spread_cores(0)
    total = logits(0)
    for copy in last:
        copy.wait_recv()
    freq = []
    for v in (0, 1):
        whole = total[v] + RX[0, v].astype(F32) + RX[1, v].astype(F32)
        saturated = jnp.log1p(jnp.maximum(whole, 0.0))
        freq.append(jnp.dot(one_hot, saturated, precision=highest, preferred_element_type=F32))
    FS[...] = jnp.where(odd == 0, freq[1], freq[0])
    FR[odd] = jnp.where(odd == 0, freq[0], freq[1])
    swapped = send(FS, FR.at[odd], swap)
    swapped.wait_recv()
    freq = FR[...].reshape(PASSAGES_HERE, FR.shape[2])
    out[...] = freq * (1.2 + 1.0) / (freq + 1.2 * scale)

    for copy in singles:
        copy.wait_send()
    for send_n, units in kinds.values():
        remote(sized(units), sized(units), send_n, 0, at(dc=1)).wait_send()
    assert used[0] <= SEND_SEMS and used[1] <= RECV_SEMS, used


def local(
    tokens, expert_routes, gate_scores, w_gate, w_up, w_down, head_weight, passage_ids, doc_length
):
    vmem, anywhere = pl.BlockSpec(memory_space=pltpu.VMEM), pl.BlockSpec(memory_space=pl.ANY)
    hidden_units, terms = w_gate.shape[2], head_weight.shape[1]

    def buffer(*shape):
        return pltpu.VMEM(shape, BF16)

    return pl.pallas_call(
        kernel,
        out_shape=jax.ShapeDtypeStruct((PASSAGES_HERE, terms), F32),
        in_specs=[vmem] * 3 + [anywhere] * 4 + [vmem] * 2,
        out_specs=vmem,
        scratch_shapes=[
            buffer(1024, FEATURES),
            buffer(1024, FEATURES),
            buffer(512, FEATURES),
            buffer(512, FEATURES),
            buffer(CHUNKS, 2, CAP, 2048),
            buffer(CHUNKS, 2, CAP, 2048),
            buffer(CHUNKS, 2, CAP, FEATURES),
            buffer(CHUNKS, 2, 64, 512),
            buffer(CHUNKS, 2, 64, 512),
            buffer(CHUNKS, 2, 64, WIDTH),
            buffer(CHUNKS, CAP, FEATURES),
            buffer(CHUNKS, 64, WIDTH),
            buffer(CHUNKS, 3, CAP, WIDTH),
            buffer(CHUNKS, 3, CAP, WIDTH),
            buffer(CHUNKS, 2, CAP, WIDTH),
            buffer(EXPERTS * CAP, WIDTH),
            buffer(EXPERTS * CAP, WIDTH),
            buffer(hidden_units, FEATURES),
            buffer(hidden_units, FEATURES),
            buffer(hidden_units, FEATURES),
            buffer(2, terms, WIDTH),
            buffer(4, 4, 2, TOK, WIDTH),
            buffer(3, 2, 256, terms),
            buffer(2, 256, terms),
            buffer(2, 2, 256, terms),
            pltpu.VMEM((32, terms), F32),
            pltpu.VMEM((2, 32, terms), F32),
            pltpu.SemaphoreType.DMA((SEND_SEMS,)),
            pltpu.SemaphoreType.DMA((RECV_SEMS,)),
            pltpu.SemaphoreType.DMA((4,)),
        ],
        compiler_params=pltpu.CompilerParams(
            collective_id=0, has_side_effects=True, vmem_limit_bytes=60 * 2**20
        ),
        cost_estimate=pl.CostEstimate(
            flops=14_000_000_000, bytes_accessed=13_000_000, transcendentals=800_000
        ),
    )(
        tokens,
        expert_routes.T,
        gate_scores.T,
        w_gate[0].T,
        w_up[0].T,
        w_down[0],
        head_weight.T,
        passage_ids.T,
        doc_length.T,
    )


def solution(mesh):
    in_specs = (
        P("exp", "voc"),
        P("exp", None),
        P("exp", None),
        P("exp", None, "voc"),
        P("exp", None, "voc"),
        P("exp", "voc", None),
        P("voc", "exp"),
        P(),
        P(),
    )
    return jax.shard_map(
        local, mesh=mesh, in_specs=in_specs, out_specs=P("voc", "exp"), check_vma=False
    )
```

time: 149 us -> 122 us (0.82)
  Pallas kernels: 147 us -> 120 us
    pallas_call x1, Pallas kernels: 147 us -> 120 us  [local(): pl.pallas_call(kernel, out_shape=jax.ShapeDtypeStruct((PASSAGES_HERE, ter...]
where the time goes in v2:
time: 122 us
  Pallas kernels  120 us (98%)
  local copies, waits for them, and re-layouts  1.57 us (1%)
    pallas_call x1, Pallas kernels, local(): pl.pallas_call(kernel, out_shape=jax.ShapeDtypeStruct((PASSAGES_HERE, ter...  120 us

profile of v2, /device:TPU:1, one launch (start us, length us, event | category | flops | bytes accessed | tf_op | source)
XLA Modules:
  0.0 122.1 jit_solution(456308583946362434)
XLA Ops:
  0.0 120.5 %shard_map.91 = f32[64,500]{1,0:T(8,128)} custom-call(bf16[32,1024]{1,0:T(8,128)(2,1)} %tok.1, s32[2,32]{1,0:T(2,128)} %bitcast.18, f32[2,32]{1,0:T(2,128)} %bitcast.19, bf16[448,4096]{1,0:T(8,128)(2,1)} %bitcast.12, bf16[448,4096]{1,0:T(8,128)(2,1)} %bitcast.13, bf16[448,4096]{1,0:T(8,128)(2,1)} %bitcast.14, bf16[500,1024]{1,0:T(8,128)(2,1)} %bitcast.15, ...), custom_call_target="tpu_custom_call" | custom-call | flops 14000000000 | bytes 13000000 | tf_op jit(solution)/shard_map/pallas_call | solution.py:423
  120.5 1.6 %copy.11 = f32[64,500]{1,0:T(8,128)} copy(f32[64,500]{1,0:T(8,128)} %shard_map.91) | data formatting | bytes 256000

commit v3 on v2

--- a/solution.py
+++ b/solution.py
@@ -16,8 +16,8 @@
 FEATURES = 4096
 CHUNKS = 4
 PASSAGES_HERE = 64
-SEND_SEMS = 22
-RECV_SEMS = 66
+SEND_SEMS = 24
+RECV_SEMS = 84
 NT = (((1,), (1,)), ((), ()))
 
 
@@ -162,42 +162,53 @@
             block = X.at[rows(k, 1, c, 0, 64), half_cols(came, half)]
             moves.append((block, block, at(dx=goes)))
         ar[k] = stage("ar", moves)
+        a3[k] = [to_core("ac", k, (0, 1, 3))]
+
+    def to_core(kind, k, steps):
+        blocks = [X.at[rows(k, 0, c, y + i, CAP), :] for i in steps]
+        blocks += [X.at[rows(k, 1, c, 0, 64), cols(i)] for i in steps]
+        return stage(kind, [(block, block, at(dc=1)) for block in blocks])
 
     def gather_cores(k):
         arrived(ar[k])
-        blocks = [X.at[rows(k, u, c, 0, 64), :] for u in (0, 1)]
-        a3[k] = stage("a3", [(block, block, at(dc=1)) for block in blocks])
+        a3[k].append(to_core("a3", k, (2,)))
 
     hidden = {}
 
     def gate_up(k):
-        arrived(a3[k])
+        for done in a3[k]:
+            arrived(done)
         here = X[k * 256 : (k + 1) * 256, :]
         gate_pre = lax.dot_general(here, WG[...], NT, preferred_element_type=F32)
         up_pre = lax.dot_general(here, WU[...], NT, preferred_element_type=F32)
         hidden[k] = (gate_pre / (1.0 + jnp.exp(-gate_pre)) * up_pre).astype(BF16)
 
     def down(k):
+        d1[k] = []
         for n in range(4):
             part = slice(n * WIDTH, (n + 1) * WIDTH)
             PART[k * 256 : (k + 1) * 256, part] = jnp.dot(
                 hidden[k], WD[:, part], preferred_element_type=F32
             ).astype(BF16)
-        d1[k] = stage("d1", [
-            (PART.at[rows(k, u, 1 - c, 0, 64), :], PREC.at[pl.ds((k * 2 + u) * 64, 64), :], at(dc=1))
-            for u in (0, 1)
-        ])
+            part = pl.ds(n * WIDTH, WIDTH)
+            moves = []
+            for u in (0, 1):
+                to = PREC.at[pl.ds((k * 2 + u) * 64, 64), part]
+                moves.append((PART.at[rows(k, u, 1 - c, 0, 64), part], to, at(dc=1)))
+            d1[k].append(stage("d1", moves))
 
     def s_rows(k, i):
         return span(k * 128 + ((y + i) % 4) * CAP, CAP)
 
     def reduce_first(k):
-        arrived(d1[k])
-        for u in (0, 1):
-            to = pl.ds((k * 2 + u) * 64, 64)
-            S[to, :] = (
-                PART[rows(k, u, c, 0, 64), :].astype(F32) + PREC[to, :].astype(F32)
-            ).astype(BF16)
+        for n in range(4):
+            arrived(d1[k][n])
+            part = slice(n * WIDTH, (n + 1) * WIDTH)
+            for u in (0, 1):
+                to = pl.ds((k * 2 + u) * 64, 64)
+                S[to, part] = (
+                    PART[rows(k, u, c, 0, 64), part].astype(F32) + PREC[to, part].astype(F32)
+                ).astype(BF16)
         s64 = pl.ds(k * 128 + 64, 64)
         moves, direct = [], []
         for half, goes in enumerate((1, 3)):
@@ -285,23 +296,23 @@
     down(1)
     gate_up(2)
     gather_cores(3)
+    down(2)
     reduce_first(1)
     reduce_relay(0)
-    down(2)
     gate_up(3)
+    down(3)
     reduce_first(2)
+    reduce_relay(1)
     reduce_second(0)
-    reduce_relay(1)
-    down(3)
+    reduce_first(3)
+    reduce_relay(2)
     reduce_second(1)
-    reduce_relay(2)
+    reduce_relay(3)
     give_back(0)
-    reduce_first(3)
+    reduce_second(2)
     give_back(1)
-    reduce_second(2)
-    reduce_relay(3)
+    reduce_second(3)
     give_back(2)
-    reduce_second(3)
     give_back(3)
 
     eye = (
@@ -316,7 +327,14 @@
     LG[z // 2, y, c] = (tok[...].astype(F32) + moe).astype(BF16)
 
     ours = LG.at[z // 2, y, c]
-    to_planes = stage("l0", [(ours, ours, at(dz=d)) for d in (4, 2, 6)])
+    turn = (z // 2 - x + 4) % 4
+    l0_send, l0_recv = fresh(0), [fresh(1) for _ in range(4)]
+
+    def to_planes():
+        for d in (4, 2, 6):
+            remote(ours, ours, l0_send, l0_recv[0] + turn, at(dz=d)).start()
+
+    pl.when(turn == 2)(to_planes)
 
     def picks(count, first_shard):
         passage = lax.broadcasted_iota(jnp.int32, (count, 64), 0)
@@ -335,6 +353,7 @@
     passage = lax.broadcasted_iota(jnp.int32, (32, 256), 0)
     token = lax.broadcasted_iota(jnp.int32, (32, 256), 1)
     one_hot = ((ids_of == (passage % 4).astype(F32)) & (token // TOK == passage // 4)).astype(F32)
+    pl.when(turn != 2)(to_planes)
     words = lengths[...].astype(F32)
     average = jnp.sum(words) / 256.0
     words = lax.dot_general(
@@ -345,12 +364,15 @@
     words = jnp.sum(jnp.where(which == passage % 4, words, 0.0), axis=1, keepdims=True)
     scale = 1.0 - 0.75 + 0.75 * words / average
 
-    head_copy.wait_recv()
-    arrived(to_planes)
     h1, h2 = {}, {}
 
     def spread_first(i):
         block = LG.at[(x + i) % 4, y, c]
+
+        @pl.when(turn != i)
+        def _():
+            remote(block, block, l0_send, l0_recv[i], at(dz=2)).wait_recv()
+
         h1[i] = stage("h1", [(block, block, at(dy=n)) for n in (2, 1, 3)])
 
     def spread_cores(i):
@@ -365,15 +387,16 @@
 
     spread_first(2)
     spread_first(1)
+    head_copy.wait_recv()
     spread_cores(2)
-    spread_first(3)
     part = logits(2)
     halfway = []
     for v, goes in enumerate((1, 3)):
         LS[0, v] = part[v].astype(BF16)
         halfway.append(send(LS.at[0, v], QX.at[v], at(dx=goes)))
+    spread_first(3)
+    spread_first(0)
     spread_cores(1)
-    spread_first(0)
     part = logits(1)
     last = []
     LS[1, 1] = part[1].astype(BF16)
@@ -392,20 +415,22 @@
     total = logits(0)
     for copy in last:
         copy.wait_recv()
-    freq = []
-    for v in (0, 1):
-        whole = total[v] + RX[0, v].astype(F32) + RX[1, v].astype(F32)
-        saturated = jnp.log1p(jnp.maximum(whole, 0.0))
-        freq.append(jnp.dot(one_hot, saturated, precision=highest, preferred_element_type=F32))
-    FS[...] = jnp.where(odd == 0, freq[1], freq[0])
-    FR[odd] = jnp.where(odd == 0, freq[0], freq[1])
+    whole = [total[v] + RX[0, v].astype(F32) + RX[1, v].astype(F32) for v in (0, 1)]
+
+    def counts(logits_of):
+        saturated = jnp.log1p(jnp.maximum(logits_of, 0.0))
+        return jnp.dot(one_hot, saturated, precision=highest, preferred_element_type=F32)
+
+    FS[...] = counts(jnp.where(odd == 0, whole[1], whole[0]))
     swapped = send(FS, FR.at[odd], swap)
+    FR[odd] = counts(jnp.where(odd == 0, whole[0], whole[1]))
     swapped.wait_recv()
     freq = FR[...].reshape(PASSAGES_HERE, FR.shape[2])
     out[...] = freq * (1.2 + 1.0) / (freq + 1.2 * scale)
 
     for copy in singles:
         copy.wait_send()
+    remote(sized(6), sized(6), l0_send, 0, at(dc=1)).wait_send()
     for send_n, units in kinds.values():
         remote(sized(units), sized(units), send_n, 0, at(dc=1)).wait_send()
     assert used[0] <= SEND_SEMS and used[1] <= RECV_SEMS, used

time: 122 us -> 118 us (0.967)
  Pallas kernels: 120 us -> 116 us
    pallas_call x1, Pallas kernels: 120 us -> 116 us  [local(): pl.pallas_call(kernel, out_shape=jax.ShapeDtypeStruct((PASSAGES_HERE, ter...]
where the time goes in v3:
time: 118 us
  Pallas kernels  116 us (98%)
  local copies, waits for them, and re-layouts  1.57 us (1%)
    pallas_call x1, Pallas kernels, local(): pl.pallas_call(kernel, out_shape=jax.ShapeDtypeStruct((PASSAGES_HERE, ter...  116 us

profile of v3, /device:TPU:1, one launch (start us, length us, event | category | flops | bytes accessed | tf_op | source)
XLA Modules:
  0.0 117.5 jit_solution(3883418017028401915)
XLA Ops:
  0.0 116.0 %shard_map.91 = f32[64,500]{1,0:T(8,128)} custom-call(bf16[32,1024]{1,0:T(8,128)(2,1)} %tok.1, s32[2,32]{1,0:T(2,128)} %bitcast.18, f32[2,32]{1,0:T(2,128)} %bitcast.19, bf16[448,4096]{1,0:T(8,128)(2,1)} %bitcast.12, bf16[448,4096]{1,0:T(8,128)(2,1)} %bitcast.13, bf16[448,4096]{1,0:T(8,128)(2,1)} %bitcast.14, bf16[500,1024]{1,0:T(8,128)(2,1)} %bitcast.15, ...), custom_call_target="tpu_custom_call" | custom-call | flops 14000000000 | bytes 13000000 | tf_op jit(solution)/shard_map/pallas_call | solution.py:448
  116.0 1.6 %copy.11 = f32[64,500]{1,0:T(8,128)} copy(f32[64,500]{1,0:T(8,128)} %shard_map.91) | data formatting | bytes 256000

commit v4 on v3

--- a/solution.py
+++ b/solution.py
@@ -302,16 +302,16 @@
     gate_up(3)
     down(3)
     reduce_first(2)
+    reduce_first(3)
     reduce_relay(1)
     reduce_second(0)
-    reduce_first(3)
     reduce_relay(2)
+    reduce_relay(3)
     reduce_second(1)
-    reduce_relay(3)
     give_back(0)
     reduce_second(2)
+    reduce_second(3)
     give_back(1)
-    reduce_second(3)
     give_back(2)
     give_back(3)
 

time: 118 us -> 117 us (level)
  no operation moved by 1% of the time
where the time goes in v4:
time: 117 us
  Pallas kernels  115 us (98%)
  local copies, waits for them, and re-layouts  1.57 us (1%)
    pallas_call x1, Pallas kernels, local(): pl.pallas_call(kernel, out_shape=jax.ShapeDtypeStruct((PASSAGES_HERE, ter...  115 us

profile of v4, /device:TPU:1, one launch (start us, length us, event | category | flops | bytes accessed | tf_op | source)
XLA Modules:
  0.0 117.1 jit_solution(12603420601845585323)
XLA Ops:
  0.0 115.5 %shard_map.91 = f32[64,500]{1,0:T(8,128)} custom-call(bf16[32,1024]{1,0:T(8,128)(2,1)} %tok.1, s32[2,32]{1,0:T(2,128)} %bitcast.18, f32[2,32]{1,0:T(2,128)} %bitcast.19, bf16[448,4096]{1,0:T(8,128)(2,1)} %bitcast.12, bf16[448,4096]{1,0:T(8,128)(2,1)} %bitcast.13, bf16[448,4096]{1,0:T(8,128)(2,1)} %bitcast.14, bf16[500,1024]{1,0:T(8,128)(2,1)} %bitcast.15, ...), custom_call_target="tpu_custom_call" | custom-call | flops 14000000000 | bytes 13000000 | tf_op jit(solution)/shard_map/pallas_call | solution.py:448
  115.5 1.6 %copy.11 = f32[64,500]{1,0:T(8,128)} copy(f32[64,500]{1,0:T(8,128)} %shard_map.91) | data formatting | bytes 256000
